TPU v7x, 32 devices: a whole 2x2x4 slice. The times are simulated.
32 devices in a mesh: groups: 2 (over x), chan: 16 (over z, y, core).
Axes of the slice: x: 2, y: 2, z: 4, core: 2. Of those that a mesh axis runs over, the one named last changes fastest.
Arguments:
- traces: float32 [1024, 4, 2048], P(('groups', 'chan')), parts along dimension 0, may hold values from -60 to 60
- fir_taps: float32 [32], replicated, may hold values from -1 to 1
- pair_list: int32 [64, 4, 256], P('groups'), parts along dimension 0, may hold values from 0 to 32767, as said below
- owners: int32 [64, 1], P('groups'), parts along dimension 0, may hold values from 0 to 15; in each aligned block of 32 rows (0 to 31, 32 to 63, ...) at most 8 rows name the same one
Outputs:
- gathers: float32 [256, 4, 256], P(('groups', 'chan')), parts along dimension 0
There are 2 independent parts, one for each index of `groups`. A program takes and returns all parts, laid end to end along the dimension named above; an argument that names none is the same for every part. Nothing has to cross between parts.
Inputs may be any that keep to these rules, and one draw needn't show every extreme that they name: `pair_list`: every pair id appears exactly once in the list. `owners`: no owner holds more than 8 virtual sources, some owner holds exactly 8, and every block owns at least one.
All inputs are finite; a program needn't handle non-finite values.
Results may differ from a plain program's by a relative error of at most 0.0033.
Values may be sent and summed in bfloat16 or wider, within the bound.
A program may use at most 64 MiB of HBM per device.

v0:
```python
import jax
import jax.numpy as jnp
from jax import lax
from jax.experimental import pallas as pl
from jax.experimental.pallas import tpu as pltpu
from jax.sharding import PartitionSpec as P

NWIN = 4
WLEN = 2048
LAGS = 256
TAPS = 32
CAP = 8
PHASES = 8
TILE = 128


epsilon = 1e-06


def shifted(value, axis, by):
    count = lax.axis_size(axis)
    return lax.ppermute(value, axis, [(i, (i + by) % count) for i in range(count)])


def whiten(traces, fir_taps):
    chans, wins, length = traces.shape
    tiles = traces.reshape(chans * wins, length // TILE, TILE)
    before = jnp.pad(tiles, ((0, 0), (1, 0), (0, 0)))[:, :-1]
    stretch = jnp.concatenate([before, tiles], axis=2)
    lag = TILE + jnp.arange(TILE)[None, :] - jnp.arange(2 * TILE)[:, None]
    hot = lag[:, :, None] == jnp.arange(TAPS)[None, None, :]
    band = jnp.sum(jnp.where(hot, fir_taps[None, None, :], 0.0), axis=2)
    filtered = jnp.einsum("rbk,kt->rbt", stretch, band, precision=lax.Precision.HIGHEST)
    signal_power = jnp.mean(filtered * filtered, axis=(1, 2), keepdims=True)
    white = (filtered * lax.rsqrt(signal_power + epsilon)).astype(jnp.bfloat16)
    white = white.reshape(chans, wins, length // PHASES, PHASES)
    return white.transpose(2, 1, 3, 0).reshape(length // PHASES * wins, PHASES * chans)


def correlation_kernel(own_ref, partner_ref, out_ref, product_ref):
    depth, width = own_ref.shape[1], own_ref.shape[0]
    chans = width // PHASES
    norm_factor = 1.0 / (NWIN * WLEN) ** 0.5
    lane = lax.broadcasted_iota(jnp.int32, (chans, width), 1)

    def product(copy, begin):
        rows = partner_ref[0, copy, pl.ds(begin, depth), :]
        return jnp.dot(own_ref[...], rows, preferred_element_type=jnp.float32)

    product_ref[0] = product(0, 0)

    def step(quad, carry):
        for r in range(4):
            d = r + 1
            now, later = r % 2, (r + 1) % 2
            begin = pl.multiple_of((quad + d // 4) * 16, 16)
            product_ref[later] = product(d % 4, begin)
            total = product_ref[now, 0:chans, :]
            for v in range(1, PHASES):
                rows = pl.ds(v * chans, chans)
                mixed = jnp.where(
                    lane < v * chans, product_ref[later, rows, :], product_ref[now, rows, :]
                )
                total = total + pltpu.roll(mixed, width - v * chans, 1)
            out_ref[0, quad * 4 + r] = total * norm_factor
        return carry

    lax.fori_loop(0, LAGS // PHASES // 4, step, 0)


def correlate(own, partners):
    depth, width = own.shape
    steps = LAGS // PHASES
    chans = width // PHASES
    rows = depth + steps * NWIN
    padded = jnp.pad(partners, ((0, 0), (0, rows - depth + 16), (0, 0)))
    copies = jnp.stack([padded[:, 4 * r : 4 * r + rows] for r in range(4)], axis=1)
    return pl.pallas_call(
        correlation_kernel,
        grid=(2,),
        out_shape=jax.ShapeDtypeStruct((2, steps, chans, width), jnp.float32),
        in_specs=[
            pl.BlockSpec((width, depth), lambda s: (0, 0)),
            pl.BlockSpec((1, 4, rows, width), lambda s: (s, 0, 0, 0)),
        ],
        out_specs=pl.BlockSpec((1, steps, chans, width), lambda s: (s, 0, 0, 0)),
        scratch_shapes=[pltpu.VMEM((2, width, width), jnp.float32)],
        compiler_params=pltpu.CompilerParams(vmem_limit_bytes=40 * 2**20),
        cost_estimate=pl.CostEstimate(
            flops=4 * (steps + 1) * width * width * depth, bytes_accessed=8 * 2**20, transcendentals=0
        ),
        name="correlation",
    )(own.T, copies)


def membership_kernel(ids_ref, out_ref):
    bins, per_bin = ids_ref.shape
    high_count, low_count = out_ref.shape[1:]
    high_ids = lax.broadcasted_iota(jnp.int32, (high_count, per_bin), 0)
    low_ids = lax.broadcasted_iota(jnp.int32, (low_count, per_bin), 0)
    for b in range(bins):
        ids = ids_ref[b : b + 1, :]
        high = jnp.where(high_ids == (ids >> 5), 1.0, 0.0).astype(jnp.bfloat16)
        low = jnp.where(low_ids == (ids & 31), 1.0, 0.0).astype(jnp.bfloat16)
        out_ref[b] = lax.dot_general(
            high, low, (((1,), (1,)), ((), ())), preferred_element_type=jnp.float32
        )


def membership(relative, high_count, low_count):
    bins, per_bin = relative.shape
    block = 16
    return pl.pallas_call(
        membership_kernel,
        grid=(bins // block,),
        out_shape=jax.ShapeDtypeStruct((bins, high_count, low_count), jnp.float32),
        in_specs=[pl.BlockSpec((block, per_bin), lambda b: (b, 0))],
        out_specs=pl.BlockSpec((block, high_count, low_count), lambda b: (b, 0, 0)),
        cost_estimate=pl.CostEstimate(
            flops=2 * bins * per_bin * high_count * 128, bytes_accessed=4 * 2**20, transcendentals=0
        ),
        name="membership",
    )(relative)


def source_slots(owners):
    owner_ids = owners[:, 0]
    positions = jnp.arange(owner_ids.shape[0], dtype=jnp.int32)
    same_owner = owner_ids[:, None] == owner_ids[None, :]
    earlier = positions[None, :] < positions[:, None]
    source_rank = jnp.sum((same_owner & earlier).astype(jnp.int32), axis=1)
    return owner_ids * CAP + source_rank


def local(traces, fir_taps, pair_list, owners):
    device_index = lax.axis_index("chan")
    chans = traces.shape[0]
    own = whiten(traces, fir_taps)
    partners = jnp.stack([shifted(own, "chan", -1), shifted(own, "chan", -2)])
    corr = correlate(own, partners)
    steps = LAGS // PHASES
    pair_table = corr.reshape(2, steps, chans, PHASES, chans).transpose(0, 4, 2, 1, 3)
    pairs_here = 2 * chans * chans
    pair_table = pair_table.reshape(pairs_here, LAGS)
    source_count, bin_width, per_bin = pair_list.shape
    relative = pair_list.reshape(source_count * bin_width, per_bin) - device_index * pairs_here
    onehot = membership(relative, 2 * chans, chans).reshape(source_count * bin_width, pairs_here)
    stacked = jnp.dot(
        onehot, pair_table, precision=lax.Precision.HIGHEST, preferred_element_type=jnp.float32
    )
    slot_of = source_slots(owners)
    wanted = jnp.arange(lax.axis_size("chan") * CAP, dtype=jnp.int32)
    select = (slot_of[None, :] == wanted[:, None]).astype(jnp.float32)
    placed = jnp.dot(
        select, stacked.reshape(source_count, bin_width * LAGS), precision=lax.Precision.HIGHEST
    ).reshape(-1, bin_width, LAGS)
    return lax.psum_scatter(placed, "chan", scatter_dimension=0, tiled=True)


def solution(mesh):
    in_specs = (P(("groups", "chan"), None, None), P(), P("groups", None, None), P("groups", None))
    out_specs = P(("groups", "chan"), None, None)
    return jax.shard_map(local, mesh=mesh, in_specs=in_specs, out_specs=out_specs, check_vma=False)
```

profile of v0, /device:TPU:0, one launch (start us, length us, event | category | flops | bytes accessed | tf_op | source)
XLA Modules:
  0.0 168.8 jit_solution(10818888368412036421)
XLA Ops:
  6.5 1.8 %reshape.69 = f32[128,16,128]{2,1,0:T(8,128)S(1)} reshape(f32[32,4,2048]{2,1,0:T(4,128)} %param.4) | data formatting | bytes 2097152 | tf_op jit(solution)/shard_map/reshape | solution.py:27
  8.3 0.0 copy-start.2
  8.3 0.3 copy.24
  8.7 0.1 pad_slice_fusion
  8.8 0.2 copy-done.2
  9.0 1.5 select_reduce_fusion
  10.4 2.4 %multiply_reduce_fusion = (f32[128]{0:T(128)S(1)}, f32[128,16,128]{0,2,1:T(8,128)S(1)}) fusion(f32[256,128]{1,0:T(8,128)S(1)} %select_reduce_fusion, f32[128,16,128]{2,0,1:T(8,128)S(1)} %copy.24, f32[128,16,128]{2,0,1:T(8,128)S(1)} %pad_slice_fusion), kind=kOutput, calls=%fused_computation.17 | convolution fusion | flops 806354816 | bytes 3277312 | tf_op jit(solution)/shard_map/rbk,kt->rbt/dot_general | solution.py:33
  12.8 0.1 multiply_convert_fusion
  13.0 0.4 copy.27
  13.4 10.5 %reshape.70 = bf16[32,4,256,8]{3,2,1,0:T(8,128)(2,1)} reshape(bf16[128,16,128]{2,1,0:T(8,128)(2,1)S(1)} %copy.27) | data formatting | bytes 1048576 | tf_op jit(solution)/shard_map/reshape | solution.py:36
  23.9 15.8 %copy.28 = bf16[256,4,8,32]{3,2,1,0:T(8,128)(2,1)S(1)} copy(bf16[256,4,8,32]{2,0,1,3:T(8,128)(2,1)} %bitcast.48) | data formatting | bytes 1048576 | tf_op jit(solution)/shard_map/transpose | solution.py:37
  39.7 1.5 reshape.71
  41.2 5.5 %collective-permute-start = (bf16[1024,256]{1,0:T(8,128)(2,1)S(1)}, bf16[1024,256]{1,0:T(8,128)(2,1)S(1)}, u32[]{:S(2)}, u32[]{:S(2)}) collective-permute-start(bf16[1024,256]{1,0:T(8,128)(2,1)S(1)} %reshape.71), channel_id=1, source_target_pairs={{0,15},{1,0},{2,1},{3,2},{4,3},{5,4},{6,5},{7,6},{8,7},{9,8},{10,9... | collective-permute-start | bytes 1572872 | tf_op jit(solution)/shard_map/ppermute | solution.py:22
  46.7 0.8 collective-permute-start.1
  47.5 0.2 copy.29
  47.8 0.7 sub.27.ids_ref
  48.4 5.8 %membership.1 = f32[128,64,32]{2,1,0:T(8,128)} custom-call(s32[128,256]{1,0:T(8,128)} %sub.27.ids_ref), custom_call_target="tpu_custom_call" | custom-call | flops 536870912 | bytes 4194304 | tf_op jit(solution)/shard_map/membership/pallas_call | solution.py:113
  54.3 4.6 %copy.23 = f32[128,64,32]{0,2,1:T(8,128)} copy(f32[128,64,32]{2,1,0:T(8,128)} %membership.1) | data formatting | bytes 2097152 | tf_op jit(solution)/shard_map/membership/pallas_call | solution.py:113
  58.9 0.2 convert_reduce_fusion
  59.1 5.6 %collective-permute-done.1 = bf16[1024,256]{1,0:T(8,128)(2,1)S(1)} collective-permute-done((bf16[1024,256]{1,0:T(8,128)(2,1)S(1)}, bf16[1024,256]{1,0:T(8,128)(2,1)S(1)}, u32[]{:S(2)}, u32[]{:S(2)}) %collective-permute-start.1) | collective-permute-done | bytes 524320 | tf_op jit(solution)/shard_map/ppermute | solution.py:22
  64.6 0.1 fusion.6
  64.7 0.4 slice_bitcast_fusion.3
  65.1 0.6 pad_maximum_fusion.partner_ref
  65.8 13.9 %correlation.1 = f32[2,32,32,256]{3,2,1,0:T(8,128)S(1)} custom-call(bf16[256,1024]{1,0:T(8,128)(2,1)S(1)} %bitcast.47, bf16[2,4,1152,256]{3,2,1,0:T(8,128)(2,1)S(1)} %pad_maximum_fusion.partner_ref), custom_call_target="tpu_custom_call" | custom-call | flops 8858370048 | bytes 8388608 | tf_op jit(solution)/shard_map/correlation/pallas_call | solution.py:78
  79.7 4.3 %reshape.72 = f32[2,32,32,8,32]{4,3,2,1,0:T(8,128)} reshape(f32[2,32,32,256]{3,2,1,0:T(8,128)S(1)} %correlation.1) | data formatting | bytes 4194304 | tf_op jit(solution)/shard_map/reshape | solution.py:142
  84.0 9.0 %copy.33 = f32[2,32,32,8,32]{2,4,0,3,1:T(8,128)} copy(f32[2,32,32,8,32]{4,3,2,1,0:T(8,128)} %reshape.72) | data formatting | bytes 4194304 | tf_op jit(solution)/shard_map/reshape | solution.py:142
  93.0 6.5 %reshape.73 = f32[2048,256]{0,1:T(8,128)S(1)} reshape(f32[2,32,32,32,8]{2,1,0,4,3:T(8,128)} %bitcast.49) | data formatting | bytes 4194304 | tf_op jit(solution)/shard_map/reshape | solution.py:144
  99.6 1.8 %fusion.16 = f32[128,256]{1,0:T(8,128)S(1)} fusion(f32[128,2048]{0,1:T(8,128)S(1)} %bitcast.50, f32[2048,256]{0,1:T(8,128)S(1)} %reshape.73), kind=kOutput, calls=%fused_computation.34 | convolution fusion | flops 805306368 | bytes 3276800 | tf_op jit(solution)/shard_map/dot_general | solution.py:148
  101.5 1.3 fusion.7
  102.7 0.0 reduce-scatter.2.cloned.1.call-update
  102.8 57.8 %reduce-scatter.2.cloned.1.call-done = f32[8,4,256]{2,0,1:T(8,128)} async-done(((f32[128,4,256]{2,0,1:T(8,128)}), f32[8,4,256]{2,0,1:T(8,128)}) %reduce-scatter.2.cloned.1.call-update) | async-done | bytes 32784 | tf_op jit(solution)/shard_map/reduce_scatter | solution.py:157
  160.6 1.4 copy.35
  (14 shorter events, 0.1 us)
Async XLA Ops:
  6.5 154.0 %reduce-scatter.2.cloned.1.call-start = ((), (), s32[]{:S(2)}) async-start(), calls=%async_computation.1 | async-start | bytes 557056 | tf_op jit(solution)/shard_map/reduce_scatter | solution.py:157
  8.3 0.7 copy-start.2
  39.7 8.0 %copy-start.1 = (s32[32,4,256]{2,1,0:T(4,128)S(1)}, s32[32,4,256]{2,1,0:T(4,128)}, u32[]{:S(2)}) copy-start(s32[32,4,256]{2,1,0:T(4,128)} %param.6) | copy-start | bytes 393220
  41.2 17.8 %collective-permute-start = (bf16[1024,256]{1,0:T(8,128)(2,1)S(1)}, bf16[1024,256]{1,0:T(8,128)(2,1)S(1)}, u32[]{:S(2)}, u32[]{:S(2)}) collective-permute-start(bf16[1024,256]{1,0:T(8,128)(2,1)S(1)} %reshape.71), channel_id=1, source_target_pairs={{0,15},{1,0},{2,1},{3,2},{4,3},{5,4},{6,5},{7,6},{8,7},{9,8},{10,9... | collective-permute-start | bytes 1572872 | tf_op jit(solution)/shard_map/ppermute | solution.py:22
  46.7 17.9 %collective-permute-start.1 = (bf16[1024,256]{1,0:T(8,128)(2,1)S(1)}, bf16[1024,256]{1,0:T(8,128)(2,1)S(1)}, u32[]{:S(2)}, u32[]{:S(2)}) collective-permute-start(bf16[1024,256]{1,0:T(8,128)(2,1)S(1)} %reshape.71), channel_id=1, source_target_pairs={{0,14},{1,15},{2,0},{3,1},{4,2},{5,3},{6,4},{7,5},{8,6},{9,7},{10,... | collective-permute-start | bytes 1572872 | tf_op jit(solution)/shard_map/ppermute | solution.py:22
  54.3 4.6 %copy-start.3 = (s32[32,1]{0,1:T(1,128)S(1)}, s32[32,1]{0,1:T(1,128)}, u32[]{:S(2)}) copy-start(s32[32,1]{0,1:T(1,128)} %param.7) | copy-start | bytes 388
  93.0 6.6 %copy-start = (f32[128,64,32]{0,2,1:T(8,128)S(1)}, f32[128,64,32]{0,2,1:T(8,128)}, u32[]{:S(2)}) copy-start(f32[128,64,32]{0,2,1:T(8,128)} %copy.23) | copy-start | bytes 3145732
Sparse Core Ops, SparseCore 0:
  102.9 57.6 reduce-scatter.1
where the time goes:
time: 170 us; the launch traced here: 169 us
  waiting for transfers between devices  63.4 us (37%)
  local copies, waits for them, and re-layouts  57.7 us (34%)
  Pallas kernels  19.8 us (12%)
  between operations  13.5 us (8%)
  starting transfers between devices  6.3 us (4%)
  matrix products  5.51 us (3%)
  other arithmetic  2.53 us (1%)
    reduce_scatter x1, waiting for transfers between devices, local(): return lax.psum_scatter(placed, 'chan', scatter_dimension=0, tiled=True)  57.8 us
    transpose x1, local copies, waits for them, and re-layouts, whiten(): white.transpose(2, 1, 3, 0).reshape(length // PHASES * wins, PHASES * chans)  15.8 us
    pallas_call x1, Pallas kernels, correlate(): pl.pallas_call(correlation_kernel, grid=(2,), out_shape=jax.ShapeDtypeStr...  13.9 us
    reshape x2, local copies, waits for them, and re-layouts, local(): corr.reshape(2, steps, chans, PHASES, chans).transpose(0, 4, 2, 1, 3)  13.3 us
    reshape x1, local copies, waits for them, and re-layouts, whiten(): white = white.reshape(chans, wins, length // PHASES, PHASES)  10.5 us
    reshape x1, local copies, waits for them, and re-layouts, local(): pair_table = pair_table.reshape(pairs_here, LAGS)  6.55 us
    ppermute x2, starting transfers between devices, shifted(): lax.ppermute(value, axis, [(i, (i + by) % count) for i in range(count)])  6.3 us
    pallas_call x1, Pallas kernels, membership(): pl.pallas_call(membership_kernel, grid=(bins // block,), out_shape=jax.Sh...  5.83 us
  transfers between devices with their start and end apart: 3, of which 2 were waited for; matrix products, arithmetic and copies ran while one was open for 3% of the time, Pallas kernels for 3%

commit v1 on v0

--- a/solution.py
+++ b/solution.py
@@ -22,19 +22,113 @@
     return lax.ppermute(value, axis, [(i, (i + by) % count) for i in range(count)])
 
 
+def whiten_kernel(traces_ref, band_ref, out_ref, filtered_ref):
+    tiles, _, rows = filtered_ref.shape
+    chans = rows // NWIN
+    ticks = TILE // PHASES
+    power = jnp.zeros((1, rows), jnp.float32)
+    for b in range(tiles):
+        block = lax.dot_general(
+            band_ref[...],
+            traces_ref[:, b * TILE : (b + 2) * TILE],
+            (((1,), (1,)), ((), ())),
+            precision=lax.Precision.HIGHEST,
+            preferred_element_type=jnp.float32,
+        )
+        filtered_ref[b] = block
+        power = power + jnp.sum(block * block, axis=0, keepdims=True)
+    scale = lax.rsqrt(power * (1.0 / WLEN) + epsilon)
+    lane = lax.broadcasted_iota(jnp.int32, (ticks, rows), 1) // chans
+
+    def place(b, carry):
+        pieces = [filtered_ref[b, v * ticks : (v + 1) * ticks, :] * scale for v in range(PHASES)]
+        begin = pl.multiple_of(b * ticks, ticks)
+        for w in range(NWIN):
+            for half in range(PHASES // NWIN):
+                total = jnp.zeros((ticks, rows), jnp.float32)
+                for c in range(NWIN):
+                    piece = pieces[half * NWIN + c]
+                    by = (c - w) * chans % rows
+                    moved = pltpu.roll(piece, by, 1) if by else piece
+                    total = jnp.where(lane == c, moved, total)
+                out_ref[w, pl.ds(begin, ticks), half * rows : (half + 1) * rows] = total.astype(
+                    jnp.bfloat16
+                )
+        return carry
+
+    lax.fori_loop(0, tiles, place, 0)
+
+
 def whiten(traces, fir_taps):
     chans, wins, length = traces.shape
-    tiles = traces.reshape(chans * wins, length // TILE, TILE)
-    before = jnp.pad(tiles, ((0, 0), (1, 0), (0, 0)))[:, :-1]
-    stretch = jnp.concatenate([before, tiles], axis=2)
-    lag = TILE + jnp.arange(TILE)[None, :] - jnp.arange(2 * TILE)[:, None]
+    rows = chans * wins
+    ordered = jnp.pad(traces.transpose(1, 0, 2).reshape(rows, length), ((0, 0), (TILE, 0)))
+    line = jnp.arange(TILE)
+    ticks = TILE // PHASES
+    when = (line % ticks) * PHASES + line // ticks
+    lag = TILE + when[:, None] - jnp.arange(2 * TILE)[None, :]
     hot = lag[:, :, None] == jnp.arange(TAPS)[None, None, :]
     band = jnp.sum(jnp.where(hot, fir_taps[None, None, :], 0.0), axis=2)
-    filtered = jnp.einsum("rbk,kt->rbt", stretch, band, precision=lax.Precision.HIGHEST)
-    signal_power = jnp.mean(filtered * filtered, axis=(1, 2), keepdims=True)
-    white = (filtered * lax.rsqrt(signal_power + epsilon)).astype(jnp.bfloat16)
-    white = white.reshape(chans, wins, length // PHASES, PHASES)
-    return white.transpose(2, 1, 3, 0).reshape(length // PHASES * wins, PHASES * chans)
+    white = pl.pallas_call(
+        whiten_kernel,
+        out_shape=jax.ShapeDtypeStruct((wins, length // PHASES, PHASES * chans), jnp.bfloat16),
+        in_specs=[pl.BlockSpec(memory_space=pltpu.VMEM)] * 2,
+        out_specs=pl.BlockSpec(memory_space=pltpu.VMEM),
+        scratch_shapes=[pltpu.VMEM((length // TILE, TILE, rows), jnp.float32)],
+        compiler_params=pltpu.CompilerParams(vmem_limit_bytes=16 * 2**20),
+        name="whitening",
+    )(ordered, band)
+    return white.transpose(1, 0, 2).reshape(length // PHASES * wins, PHASES * chans)
+
+
+def exchange_kernel(placed_ref, out_ref, arrived, send_sems, recv_sems):
+    count, rows = placed_ref.shape[:2]
+    me = lax.axis_index("chan")
+    barrier = pltpu.get_barrier_semaphore()
+    for k in range(1, count):
+        pl.semaphore_signal(
+            barrier, inc=1, device_id={"chan": lax.rem(me + k, count)}, device_id_type=pl.DeviceIdType.MESH
+        )
+    pl.semaphore_wait(barrier, count - 1)
+    copies = []
+    for k in range(1, count):
+        peer = lax.rem(me + k, count)
+        copy = pltpu.make_async_remote_copy(
+            src_ref=placed_ref.at[peer],
+            dst_ref=arrived.at[k],
+            send_sem=send_sems.at[k],
+            recv_sem=recv_sems.at[k],
+            device_id={"chan": peer},
+            device_id_type=pl.DeviceIdType.MESH,
+        )
+        copy.start()
+        copies.append(copy)
+    total = placed_ref[me]
+    for k, copy in enumerate(copies, 1):
+        copy.wait_recv()
+        total = total + arrived[k]
+    out_ref[...] = total
+    for copy in copies:
+        copy.wait_send()
+
+
+def exchange(placed):
+    count, rows, width = placed.shape
+    return pl.pallas_call(
+        exchange_kernel,
+        out_shape=jax.ShapeDtypeStruct((rows, width), jnp.float32),
+        in_specs=[pl.BlockSpec(memory_space=pltpu.VMEM)],
+        out_specs=pl.BlockSpec(memory_space=pltpu.VMEM),
+        scratch_shapes=[
+            pltpu.VMEM((count, rows, width), jnp.float32),
+            pltpu.SemaphoreType.DMA((count,)),
+            pltpu.SemaphoreType.DMA((count,)),
+        ],
+        compiler_params=pltpu.CompilerParams(
+            collective_id=0, has_side_effects=True, vmem_limit_bytes=16 * 2**20
+        ),
+        name="exchange",
+    )(placed)
 
 
 def correlation_kernel(own_ref, partner_ref, out_ref, product_ref):
@@ -153,8 +247,8 @@
     select = (slot_of[None, :] == wanted[:, None]).astype(jnp.float32)
     placed = jnp.dot(
         select, stacked.reshape(source_count, bin_width * LAGS), precision=lax.Precision.HIGHEST
-    ).reshape(-1, bin_width, LAGS)
-    return lax.psum_scatter(placed, "chan", scatter_dimension=0, tiled=True)
+    ).reshape(-1, CAP * bin_width, LAGS)
+    return exchange(placed).reshape(CAP, bin_width, LAGS)
 
 
 def solution(mesh):

time: 170 us -> 85.4 us (0.50)
  the two profiles are of different devices: /device:TPU:0 before, /device:TPU:15 now
where the time goes in v1:
time: 85.4 us; the launch traced here: 84.6 us
  Pallas kernels  46.9 us (55%)
  local copies, waits for them, and re-layouts  29 us (34%)
  waiting for transfers between devices  3.13 us (4%)
  other arithmetic  2.31 us (3%)
  matrix products  2.19 us (3%)
  starting transfers between devices  0.95 us (1%)
    pallas_call x1, Pallas kernels, exchange(): pl.pallas_call(exchange_kernel, out_shape=jax.ShapeDtypeStruct((rows, wid...  23.8 us
    pallas_call x1, Pallas kernels, correlate(): pl.pallas_call(correlation_kernel, grid=(2,), out_shape=jax.ShapeDtypeStr...  13.9 us
    reshape x2, local copies, waits for them, and re-layouts, local(): corr.reshape(2, steps, chans, PHASES, chans).transpose(0, 4, 2, 1, 3)  13.3 us
    reshape x1, local copies, waits for them, and re-layouts, local(): pair_table = pair_table.reshape(pairs_here, LAGS)  6.55 us
    pallas_call x1, Pallas kernels, membership(): pl.pallas_call(membership_kernel, grid=(bins // block,), out_shape=jax.Sh...  5.81 us
    pallas_call x1, local copies, waits for them, and re-layouts, membership(): pl.pallas_call(membership_kernel, grid=(bins // block,), out_shape=jax.Sh...  4.55 us
    pallas_call x1, Pallas kernels, whiten(): pl.pallas_call(whiten_kernel, out_shape=jax.ShapeDtypeStruct((wins, lengt...  3.39 us
    ppermute x2, waiting for transfers between devices, shifted(): lax.ppermute(value, axis, [(i, (i + by) % count) for i in range(count)])  3.13 us
  transfers between devices with their start and end apart: 2, of which 2 were waited for; matrix products, arithmetic and copies ran while one was open for 7% of the time, Pallas kernels for 7%

profile of v1, /device:TPU:15, one launch (start us, length us, event | category | flops | bytes accessed | tf_op | source)
XLA Modules:
  0.0 84.6 jit_solution(18280402779671271450)
XLA Ops:
  0.0 1.8 %copy.20 = f32[4,32,2048]{2,1,0:T(8,128)S(1)} copy(f32[4,32,2048]{2,0,1:T(4,128)} %bitcast.40) | data formatting | bytes 2097152 | tf_op jit(solution)/shard_map/transpose | solution.py:65
  1.9 0.1 iota_subtract_fusion
  1.9 0.1 pad.8.traces_ref
  2.0 0.0 copy-done.2
  2.0 1.3 %select_reduce_fusion.band_ref = f32[128,256]{1,0:T(8,128)S(1)} fusion(f32[32]{0:T(128)S(1)} %copy-done.2, s32[128,256]{1,0:T(8,128)S(1)} %iota_subtract_fusion), kind=kLoop, calls=%fused_computation.1 | loop fusion | flops 3112960 | bytes 262272 | tf_op jit(solution)/shard_map/reduce_sum | solution.py:71
  3.4 0.0 copy-start.1
  3.4 3.4 %whitening.1 = bf16[4,256,256]{2,1,0:T(8,128)(2,1)S(1)} custom-call(f32[128,2176]{1,0:T(8,128)S(1)} %pad.8.traces_ref, f32[128,256]{1,0:T(8,128)S(1)} %select_reduce_fusion.band_ref), custom_call_target="tpu_custom_call" | custom-call | tf_op jit(solution)/shard_map/whitening/pallas_call | solution.py:72
  6.8 0.4 copy.21
  7.2 0.1 reshape.83
  7.3 0.7 collective-permute-start
  8.0 0.2 collective-permute-start.1
  8.3 0.2 copy.25.own_ref
  8.5 0.0 copy-done.1
  8.5 0.7 sub.33.ids_ref
  9.2 5.8 %membership.1 = f32[128,64,32]{2,1,0:T(8,128)} custom-call(s32[128,256]{1,0:T(8,128)} %sub.33.ids_ref), custom_call_target="tpu_custom_call" | custom-call | flops 536870912 | bytes 4194304 | tf_op jit(solution)/shard_map/membership/pallas_call | solution.py:207
  15.0 4.5 %copy.19 = f32[128,64,32]{0,2,1:T(8,128)} copy(f32[128,64,32]{2,1,0:T(8,128)} %membership.1) | data formatting | bytes 2097152 | tf_op jit(solution)/shard_map/membership/pallas_call | solution.py:207
  19.6 0.0 copy-done.3
  19.6 0.2 convert_reduce_fusion
  19.7 2.6 %collective-permute-done = bf16[1024,256]{1,0:T(8,128)(2,1)S(1)} collective-permute-done((bf16[1024,256]{1,0:T(8,128)(2,1)S(1)}, bf16[1024,256]{1,0:T(8,128)(2,1)S(1)}, u32[]{:S(2)}, u32[]{:S(2)}) %collective-permute-start) | collective-permute-done | bytes 524320 | tf_op jit(solution)/shard_map/ppermute | solution.py:22
  22.4 0.5 collective-permute-done.1
  22.9 0.1 fusion.2
  23.0 0.4 slice_bitcast_fusion.3
  23.4 0.6 pad_maximum_fusion.partner_ref
  24.0 13.9 %correlation.1 = f32[2,32,32,256]{3,2,1,0:T(8,128)S(1)} custom-call(bf16[256,1024]{1,0:T(8,128)(2,1)S(1)} %copy.25.own_ref, bf16[2,4,1152,256]{3,2,1,0:T(8,128)(2,1)S(1)} %pad_maximum_fusion.partner_ref), custom_call_target="tpu_custom_call" | custom-call | flops 8858370048 | bytes 8388608 | tf_op jit(solution)/shard_map/correlation/pallas_call | solution.py:172
  37.9 4.3 %reshape.84 = f32[2,32,32,8,32]{4,3,2,1,0:T(8,128)} reshape(f32[2,32,32,256]{3,2,1,0:T(8,128)S(1)} %correlation.1) | data formatting | bytes 4194304 | tf_op jit(solution)/shard_map/reshape | solution.py:236
  42.2 9.0 %copy.26 = f32[2,32,32,8,32]{2,4,0,3,1:T(8,128)} copy(f32[2,32,32,8,32]{4,3,2,1,0:T(8,128)} %reshape.84) | data formatting | bytes 4194304 | tf_op jit(solution)/shard_map/reshape | solution.py:236
  51.2 6.5 %reshape.85 = f32[2048,256]{0,1:T(8,128)S(1)} reshape(f32[2,32,32,32,8]{2,1,0,4,3:T(8,128)} %bitcast.36) | data formatting | bytes 4194304 | tf_op jit(solution)/shard_map/reshape | solution.py:238
  57.8 1.8 %fusion.9 = f32[128,256]{1,0:T(8,128)S(1)} fusion(f32[128,2048]{0,1:T(8,128)S(1)} %bitcast.37, f32[2048,256]{0,1:T(8,128)S(1)} %reshape.85), kind=kOutput, calls=%fused_computation.28 | convolution fusion | flops 805306368 | bytes 3276800 | tf_op jit(solution)/shard_map/dot_general | solution.py:242
  59.7 0.4 fusion.3
  60.1 0.1 reshape.87.placed_ref
  60.2 23.8 %exchange.1 = f32[32,256]{1,0:T(8,128)S(1)} custom-call(f32[16,32,256]{2,1,0:T(8,128)S(1)} %reshape.87.placed_ref), custom_call_target="tpu_custom_call" | custom-call | tf_op jit(solution)/shard_map/exchange/pallas_call | solution.py:117
  84.0 0.6 reshape.88
  (8 shorter events, 0.1 us)
Async XLA Ops:
  0.0 2.0 %copy-start.2 = (f32[32]{0:T(128)S(1)}, f32[32]{0:T(128)}, u32[]{:S(2)}) copy-start(f32[32]{0:T(128)} %param.5) | copy-start | bytes 388
  3.4 5.1 %copy-start.1 = (s32[32,4,256]{2,1,0:T(4,128)S(1)}, s32[32,4,256]{2,1,0:T(4,128)}, u32[]{:S(2)}) copy-start(s32[32,4,256]{2,1,0:T(4,128)} %param.6) | copy-start | bytes 393220
  7.3 15.1 %collective-permute-start = (bf16[1024,256]{1,0:T(8,128)(2,1)S(1)}, bf16[1024,256]{1,0:T(8,128)(2,1)S(1)}, u32[]{:S(2)}, u32[]{:S(2)}) collective-permute-start(bf16[1024,256]{1,0:T(8,128)(2,1)S(1)} %reshape.83), channel_id=1, source_target_pairs={{0,15},{1,0},{2,1},{3,2},{4,3},{5,4},{6,5},{7,6},{8,7},{9,8},{10,9... | collective-permute-start | bytes 1572872 | tf_op jit(solution)/shard_map/ppermute | solution.py:22
  8.0 14.8 %collective-permute-start.1 = (bf16[1024,256]{1,0:T(8,128)(2,1)S(1)}, bf16[1024,256]{1,0:T(8,128)(2,1)S(1)}, u32[]{:S(2)}, u32[]{:S(2)}) collective-permute-start(bf16[1024,256]{1,0:T(8,128)(2,1)S(1)} %reshape.83), channel_id=1, source_target_pairs={{0,14},{1,15},{2,0},{3,1},{4,2},{5,3},{6,4},{7,5},{8,6},{9,7},{10,... | collective-permute-start | bytes 1572872 | tf_op jit(solution)/shard_map/ppermute | solution.py:22
  15.0 4.6 %copy-start.3 = (s32[32,1]{0,1:T(1,128)S(1)}, s32[32,1]{0,1:T(1,128)}, u32[]{:S(2)}) copy-start(s32[32,1]{0,1:T(1,128)} %param.7) | copy-start | bytes 388
  51.2 6.6 %copy-start = (f32[128,64,32]{0,2,1:T(8,128)S(1)}, f32[128,64,32]{0,2,1:T(8,128)}, u32[]{:S(2)}) copy-start(f32[128,64,32]{0,2,1:T(8,128)} %copy.19) | copy-start | bytes 3145732

commit v2 on v1

--- a/solution.py
+++ b/solution.py
@@ -156,7 +156,7 @@
                     lane < v * chans, product_ref[later, rows, :], product_ref[now, rows, :]
                 )
                 total = total + pltpu.roll(mixed, width - v * chans, 1)
-            out_ref[0, quad * 4 + r] = total * norm_factor
+            out_ref[0, :, quad * 4 + r, :] = total * norm_factor
         return carry
 
     lax.fori_loop(0, LAGS // PHASES // 4, step, 0)
@@ -172,12 +172,12 @@
     return pl.pallas_call(
         correlation_kernel,
         grid=(2,),
-        out_shape=jax.ShapeDtypeStruct((2, steps, chans, width), jnp.float32),
+        out_shape=jax.ShapeDtypeStruct((2, chans, steps, width), jnp.float32),
         in_specs=[
             pl.BlockSpec((width, depth), lambda s: (0, 0)),
             pl.BlockSpec((1, 4, rows, width), lambda s: (s, 0, 0, 0)),
         ],
-        out_specs=pl.BlockSpec((1, steps, chans, width), lambda s: (s, 0, 0, 0)),
+        out_specs=pl.BlockSpec((1, chans, steps, width), lambda s: (s, 0, 0, 0)),
         scratch_shapes=[pltpu.VMEM((2, width, width), jnp.float32)],
         compiler_params=pltpu.CompilerParams(vmem_limit_bytes=40 * 2**20),
         cost_estimate=pl.CostEstimate(
@@ -194,8 +194,10 @@
     low_ids = lax.broadcasted_iota(jnp.int32, (low_count, per_bin), 0)
     for b in range(bins):
         ids = ids_ref[b : b + 1, :]
-        high = jnp.where(high_ids == (ids >> 5), 1.0, 0.0).astype(jnp.bfloat16)
-        low = jnp.where(low_ids == (ids & 31), 1.0, 0.0).astype(jnp.bfloat16)
+        place = (ids & 3) * 16 + (ids >> 10) * 8 + ((ids & 31) >> 2)
+        place = jnp.where((ids >= 0) & (ids < high_count * low_count), place, -1)
+        high = jnp.where(high_ids == place, 1.0, 0.0).astype(jnp.bfloat16)
+        low = jnp.where(low_ids == ((ids >> 5) & 31), 1.0, 0.0).astype(jnp.bfloat16)
         out_ref[b] = lax.dot_general(
             high, low, (((1,), (1,)), ((), ())), preferred_element_type=jnp.float32
         )
@@ -233,15 +235,21 @@
     partners = jnp.stack([shifted(own, "chan", -1), shifted(own, "chan", -2)])
     corr = correlate(own, partners)
     steps = LAGS // PHASES
-    pair_table = corr.reshape(2, steps, chans, PHASES, chans).transpose(0, 4, 2, 1, 3)
     pairs_here = 2 * chans * chans
-    pair_table = pair_table.reshape(pairs_here, LAGS)
+    four = TILE // steps
+    turned = jnp.swapaxes(corr.reshape(2 * chans // four, TILE, PHASES * chans), 1, 2)
+    table = turned.reshape(2 * chans // four, PHASES, chans, TILE).transpose(0, 2, 1, 3)
+    table = table.reshape(pairs_here // four, PHASES * TILE)
     source_count, bin_width, per_bin = pair_list.shape
     relative = pair_list.reshape(source_count * bin_width, per_bin) - device_index * pairs_here
-    onehot = membership(relative, 2 * chans, chans).reshape(source_count * bin_width, pairs_here)
-    stacked = jnp.dot(
-        onehot, pair_table, precision=lax.Precision.HIGHEST, preferred_element_type=jnp.float32
-    )
+    bins = source_count * bin_width
+    onehot = membership(relative, 2 * chans, chans).reshape(bins * four, pairs_here // four)
+    every = jnp.dot(
+        onehot, table, precision=lax.Precision.HIGHEST, preferred_element_type=jnp.float32
+    ).reshape(bins, four, PHASES, TILE)
+    mine = (jnp.arange(TILE)[None, :] // steps) == jnp.arange(four)[:, None]
+    kept = jnp.sum(jnp.where(mine[None, :, None, :], every, 0.0), axis=1)
+    stacked = jnp.sum(kept.reshape(bins, PHASES, four, steps), axis=2).transpose(0, 2, 1)
     slot_of = source_slots(owners)
     wanted = jnp.arange(lax.axis_size("chan") * CAP, dtype=jnp.int32)
     select = (slot_of[None, :] == wanted[:, None]).astype(jnp.float32)

time: 85.4 us -> 85.2 us (level)
  local copies, waits for them, and re-layouts: 29 us -> 22.5 us
  matrix products: 2.19 us -> 7.87 us
    reshape x3 -> x1, local copies, waits for them, and re-layouts: 19.8 us -> 1.87 us  [local(): corr.reshape(2 * chans // four, TILE, PHASES * chans)]
    dot_general x1, matrix products: 1.83 us -> 7.51 us  [local(): jnp.dot(onehot, table, precision=lax.Precision.HIGHEST, preferred_element...]
    transpose x0 -> x2, local copies, waits for them, and re-layouts: none -> 5.09 us  [the longest x1 3.23 us: local(): turned.reshape(2 * chans // four, PHASES, chans, TILE).transpose(0, 2, 1, 3)]
    dot_general x0 -> x1, local copies, waits for them, and re-layouts: none -> 2.19 us  [local(): jnp.dot(onehot, table, precision=lax.Precision.HIGHEST, preferred_element...]
    unnamed x8 -> x9, local copies, waits for them, and re-layouts: 0.02 us -> 1.83 us
    reduce_sum x0 -> x1, local copies, waits for them, and re-layouts: none -> 1.24 us  [local(): kept = jnp.sum(jnp.where(mine[None, :, None, :], every, 0.0), axis=1)]
    reshape x1, local copies, waits for them, and re-layouts: 0.04 us -> 1.2 us  [local(): stacked.reshape(source_count, bin_width * LAGS)]
where the time goes in v2:
time: 85.2 us; the launch traced here: 84.6 us
  Pallas kernels  47.7 us (56%)
  local copies, waits for them, and re-layouts  22.5 us (26%)
  matrix products  7.87 us (9%)
  waiting for transfers between devices  3.01 us (4%)
  other arithmetic  2.36 us (3%)
  starting transfers between devices  0.95 us (1%)
    pallas_call x1, Pallas kernels, exchange(): pl.pallas_call(exchange_kernel, out_shape=jax.ShapeDtypeStruct((rows, wid...  23.8 us
    pallas_call x1, Pallas kernels, correlate(): pl.pallas_call(correlation_kernel, grid=(2,), out_shape=jax.ShapeDtypeStr...  14.6 us
    dot_general x1, matrix products, local(): jnp.dot(onehot, table, precision=lax.Precision.HIGHEST, preferred_element...  7.51 us
    pallas_call x1, Pallas kernels, membership(): pl.pallas_call(membership_kernel, grid=(bins // block,), out_shape=jax.Sh...  5.87 us
    pallas_call x1, local copies, waits for them, and re-layouts, membership(): pl.pallas_call(membership_kernel, grid=(bins // block,), out_shape=jax.Sh...  4.58 us
    pallas_call x1, Pallas kernels, whiten(): pl.pallas_call(whiten_kernel, out_shape=jax.ShapeDtypeStruct((wins, lengt...  3.39 us
    transpose x1, local copies, waits for them, and re-layouts, local(): turned.reshape(2 * chans // four, PHASES, chans, TILE).transpose(0, 2, 1, 3)  3.23 us
    ppermute x2, waiting for transfers between devices, shifted(): lax.ppermute(value, axis, [(i, (i + by) % count) for i in range(count)])  3.01 us
  transfers between devices with their start and end apart: 2, of which 2 were waited for; matrix products, arithmetic and copies ran while one was open for 7% of the time, Pallas kernels for 7%

profile of v2, /device:TPU:15, one launch (start us, length us, event | category | flops | bytes accessed | tf_op | source)
XLA Modules:
  0.0 84.6 jit_solution(12456868312054094063)
XLA Ops:
  0.0 1.8 %copy.38 = f32[4,32,2048]{2,1,0:T(8,128)S(1)} copy(f32[4,32,2048]{2,0,1:T(4,128)} %bitcast.61) | data formatting | bytes 2097152 | tf_op jit(solution)/shard_map/transpose | solution.py:65
  1.9 0.1 iota_subtract_fusion
  1.9 0.1 pad.8.traces_ref
  2.0 1.3 %select_reduce_fusion.band_ref = f32[128,256]{1,0:T(8,128)S(1)} fusion(f32[32]{0:T(128)S(1)} %copy-done.2, s32[128,256]{1,0:T(8,128)S(1)} %iota_subtract_fusion), kind=kLoop, calls=%fused_computation.1 | loop fusion | flops 3112960 | bytes 262272 | tf_op jit(solution)/shard_map/reduce_sum | solution.py:71
  3.4 3.4 %whitening.1 = bf16[4,256,256]{2,1,0:T(8,128)(2,1)S(1)} custom-call(f32[128,2176]{1,0:T(8,128)S(1)} %pad.8.traces_ref, f32[128,256]{1,0:T(8,128)S(1)} %select_reduce_fusion.band_ref), custom_call_target="tpu_custom_call" | custom-call | tf_op jit(solution)/shard_map/whitening/pallas_call | solution.py:72
  6.8 0.4 copy.39
  7.2 0.1 reshape.147
  7.3 0.7 collective-permute-start
  8.0 0.2 collective-permute-start.1
  8.3 0.2 copy.43.own_ref
  8.5 0.7 sub.40.ids_ref
  9.2 5.9 %membership.1 = f32[128,64,32]{2,1,0:T(8,128)} custom-call(s32[128,256]{1,0:T(8,128)} %sub.40.ids_ref), custom_call_target="tpu_custom_call" | custom-call | flops 536870912 | bytes 4194304 | tf_op jit(solution)/shard_map/membership/pallas_call | solution.py:209
  15.1 4.6 %copy.37 = f32[128,64,32]{0,2,1:T(8,128)} copy(f32[128,64,32]{2,1,0:T(8,128)} %membership.1) | data formatting | bytes 2097152 | tf_op jit(solution)/shard_map/membership/pallas_call | solution.py:209
  19.6 0.2 convert_reduce_fusion
  19.9 2.5 %collective-permute-done = bf16[1024,256]{1,0:T(8,128)(2,1)S(1)} collective-permute-done((bf16[1024,256]{1,0:T(8,128)(2,1)S(1)}, bf16[1024,256]{1,0:T(8,128)(2,1)S(1)}, u32[]{:S(2)}, u32[]{:S(2)}) %collective-permute-start) | collective-permute-done | bytes 524320 | tf_op jit(solution)/shard_map/ppermute | solution.py:22
  22.4 0.5 collective-permute-done.1
  22.9 0.1 fusion.2
  23.0 0.4 slice_bitcast_fusion.3
  23.4 0.6 pad_maximum_fusion.partner_ref
  24.0 14.6 %correlation.1 = f32[2,32,32,256]{3,2,1,0:T(8,128)S(1)} custom-call(bf16[256,1024]{1,0:T(8,128)(2,1)S(1)} %copy.43.own_ref, bf16[2,4,1152,256]{3,2,1,0:T(8,128)(2,1)S(1)} %pad_maximum_fusion.partner_ref), custom_call_target="tpu_custom_call" | custom-call | flops 8858370048 | bytes 8388608 | tf_op jit(solution)/shard_map/correlation/pallas_call | solution.py:172
  38.6 1.9 %copy.44 = f32[16,128,256]{1,2,0:T(8,128)} copy(f32[16,128,256]{2,1,0:T(8,128)S(1)} %bitcast.52) | data formatting | bytes 4194304 | tf_op jit(solution)/shard_map/reshape | solution.py:240
  40.5 3.2 %copy.45 = f32[16,32,8,128]{3,2,1,0:T(8,128)S(1)} copy(f32[16,32,8,128]{3,1,2,0:T(8,128)} %bitcast.54) | data formatting | bytes 4194304 | tf_op jit(solution)/shard_map/transpose | solution.py:241
  43.7 1.8 %copy.56 = f32[64,8,8,128]{3,1,2,0:T(8,128)} copy(f32[64,8,8,128]{3,2,1,0:T(8,128)S(1)} %bitcast.55) | data formatting | bytes 4194304
  45.6 2.2 %copy.53 = f32[1024,512]{1,0:T(8,128)S(1)} copy(f32[1024,512]{0,1:T(8,128)} %bitcast.56) | data formatting | bytes 4194304 | tf_op jit(solution)/shard_map/dot_general | solution.py:247
  47.8 7.5 %select_reduce_fusion.1 = f32[128,8,128]{2,0,1:T(8,128)} fusion(f32[128,4,512,1]{0,2,3,1:T(8,128)S(1)} %bitcast.58, f32[8,128,512,1]{2,1,0,3:T(8,128)S(1)} %bitcast.53, pred[4,128]{1,0:T(4,128)(4,1)S(1)} %iota_compare_fusion.5), kind=kOutput, calls=%fused_computation.7 | convolution fusion | flops 3222142976 | bytes 3670528 | tf_op jit(solution)/shard_map/dot_general | solution.py:247
  55.3 1.2 %copy.48 = f32[128,8,128]{0,2,1:T(8,128)S(1)} copy(f32[128,8,128]{2,0,1:T(8,128)} %select_reduce_fusion.1) | data formatting | bytes 1048576 | tf_op jit(solution)/shard_map/reduce_sum | solution.py:251
  56.6 1.9 %copy.49 = f32[128,32,8]{2,1,0:T(8,128)S(1)} copy(f32[128,32,8]{0,1,2:T(8,128)S(1)} %bitcast.64) | data formatting | bytes 262144 | tf_op jit(solution)/shard_map/transpose | solution.py:252
  58.4 1.2 %reshape.152 = f32[32,1024]{1,0:T(8,128)S(1)} reshape(f32[128,32,8]{2,1,0:T(8,128)S(1)} %copy.49) | data formatting | bytes 262144 | tf_op jit(solution)/shard_map/reshape | solution.py:257
  59.6 0.4 fusion.3
  60.0 0.1 reshape.153.placed_ref
  60.2 23.8 %exchange.1 = f32[32,256]{1,0:T(8,128)S(1)} custom-call(f32[16,32,256]{2,1,0:T(8,128)S(1)} %reshape.153.placed_ref), custom_call_target="tpu_custom_call" | custom-call | tf_op jit(solution)/shard_map/exchange/pallas_call | solution.py:117
  84.0 0.6 reshape.154
  (14 shorter events, 0.1 us)
Async XLA Ops:
  0.0 2.0 %copy-start.2 = (f32[32]{0:T(128)S(1)}, f32[32]{0:T(128)}, u32[]{:S(2)}) copy-start(f32[32]{0:T(128)} %param.5) | copy-start | bytes 388
  3.4 5.1 %copy-start.1 = (s32[32,4,256]{2,1,0:T(4,128)S(1)}, s32[32,4,256]{2,1,0:T(4,128)}, u32[]{:S(2)}) copy-start(s32[32,4,256]{2,1,0:T(4,128)} %param.6) | copy-start | bytes 393220
  7.3 15.1 %collective-permute-start = (bf16[1024,256]{1,0:T(8,128)(2,1)S(1)}, bf16[1024,256]{1,0:T(8,128)(2,1)S(1)}, u32[]{:S(2)}, u32[]{:S(2)}) collective-permute-start(bf16[1024,256]{1,0:T(8,128)(2,1)S(1)} %reshape.147), channel_id=1, source_target_pairs={{0,15},{1,0},{2,1},{3,2},{4,3},{5,4},{6,5},{7,6},{8,7},{9,8},{10,9... | collective-permute-start | bytes 1572872 | tf_op jit(solution)/shard_map/ppermute | solution.py:22
  8.0 14.8 %collective-permute-start.1 = (bf16[1024,256]{1,0:T(8,128)(2,1)S(1)}, bf16[1024,256]{1,0:T(8,128)(2,1)S(1)}, u32[]{:S(2)}, u32[]{:S(2)}) collective-permute-start(bf16[1024,256]{1,0:T(8,128)(2,1)S(1)} %reshape.147), channel_id=1, source_target_pairs={{0,14},{1,15},{2,0},{3,1},{4,2},{5,3},{6,4},{7,5},{8,6},{9,7},{10,... | collective-permute-start | bytes 1572872 | tf_op jit(solution)/shard_map/ppermute | solution.py:22
  15.1 4.6 %copy-start.3 = (s32[32,1]{0,1:T(1,128)S(1)}, s32[32,1]{0,1:T(1,128)}, u32[]{:S(2)}) copy-start(s32[32,1]{0,1:T(1,128)} %param.7) | copy-start | bytes 388
  45.6 2.2 %copy-start = (f32[128,64,32]{0,2,1:T(8,128)S(1)}, f32[128,64,32]{0,2,1:T(8,128)}, u32[]{:S(2)}) copy-start(f32[128,64,32]{0,2,1:T(8,128)} %copy.37) | copy-start | bytes 3145732
